TPU v7x, 32 devices: a whole 2x2x4 slice. The times are simulated.
32 devices in a mesh: grp: 2 (over y), wide: 8 (over z, x), narrow: 2 (over core).
Axes of the slice: x: 2, y: 2, z: 4, core: 2. Of those that a mesh axis runs over, the one named last changes fastest.
Arguments:
- traces: bfloat16 [1024, 64, 512], P('wide', ('grp', 'narrow')), parts along dimension 1, may hold values from -6 to 6
- aperture: int32 [64, 1], P(('grp', 'narrow')), parts along dimension 0, may hold values 0 or 1
- source_points: int32 [64], P('grp'), parts along dimension 0, may hold values from 0 to 511, as said below
- freq_idx: int32 [2], replicated, may hold values from 1 to 511
Outputs:
- multiples: float32 [2, 2, 64, 512], P(None, None, ('grp', 'narrow'), 'wide'), parts along dimension 2
There are 2 independent parts, one for each index of `grp`. A program takes and returns all parts, laid end to end along the dimension named above; an argument that names none is the same for every part. Nothing has to cross between parts.
Inputs may be any that keep to these rules, and one draw needn't show every extreme that they name: `source_points`: shot k stands at a receiver of k * 16 to (k + 1) * 16 - 1; the first shot at receiver 0 and the last at receiver 512 - 1.
All inputs are finite; a program needn't handle non-finite values. No bound on the sum of `aperture` on one device may be relied on, other than what follows from the above.
Results may differ from a plain program's by a relative error of at most 0.0033.
Values may be sent and summed in bfloat16 or wider, within the bound.
A program may use at most 192 MiB of HBM per device.

v0:
```python
import math

import jax
import jax.numpy as jnp
from jax import lax
from jax.sharding import PartitionSpec as P

NT = 1024
RB = 512


def dft_rows(time_samples_count, freq_rows):
    phase_index = freq_rows[:, None] * time_samples_count[None, :] % NT
    angles = 2.0 * math.pi / NT * phase_index.astype(jnp.float32)
    return jnp.concatenate([jnp.cos(angles), -jnp.sin(angles)], axis=0).astype(jnp.bfloat16)


def product_mix(left_side, right_side):
    return jnp.einsum("qsk,qkr->qsr", left_side, right_side, precision=lax.Precision.HIGHEST)


def apply_table(fourier_table, column_entries):
    return jnp.einsum(
        "ua,aid->uid", fourier_table, column_entries, preferred_element_type=jnp.float32
    )


def shards(traces, aperture, source_points, freq_idx):
    wide_count = lax.axis_size("wide")
    wide_index = lax.axis_index("wide")
    shot_count = traces.shape[1]
    recv_total = traces.shape[2]
    recv_count = recv_total // wide_count
    first_recv = wide_index * recv_count
    own_block = first_recv // RB
    block_numbers = jnp.arange(aperture.shape[1], dtype=jnp.int32)
    active_flags = jnp.sum(jnp.where(block_numbers[None, :] == own_block, aperture, 0), axis=1)
    freq_count = freq_idx.shape[0]
    column_entries = lax.all_to_all(traces, "wide", split_axis=2, concat_axis=0, tiled=True)
    fourier_table = dft_rows(jnp.arange(NT, dtype=jnp.int32), freq_idx)
    spectra = apply_table(fourier_table, column_entries)
    live_scale = active_flags.astype(jnp.float32) * NT ** (-0.5)
    spectra = (spectra * live_scale[None, :, None]).reshape(2, freq_count, shot_count, recv_count)
    station_positions = first_recv + jnp.arange(recv_count, dtype=jnp.int32)
    selector = (source_points[:, None] == station_positions[None, :]).astype(jnp.float32)
    local_part = jnp.einsum("cqsj,kj->cqsk", spectra, selector, precision=lax.Precision.HIGHEST)
    coincident = lax.psum(local_part, "wide")
    all_shot_records = lax.all_gather(spectra, "narrow", axis=2, tiled=True)
    real_part = product_mix(coincident[0], all_shot_records[0]) - product_mix(
        coincident[1], all_shot_records[1]
    )
    imag_part = product_mix(coincident[0], all_shot_records[1]) + product_mix(
        coincident[1], all_shot_records[0]
    )
    return jnp.stack([real_part, imag_part]) * source_points.shape[0] ** (-0.5)


def solution(mesh):
    placed = (P("wide", ("grp", "narrow"), None), P(("grp", "narrow"), None), P("grp"), P())
    return jax.shard_map(
        shards,
        mesh=mesh,
        in_specs=placed,
        out_specs=P(None, None, ("grp", "narrow"), "wide"),
        check_vma=False,
    )
```

profile of v0, /device:TPU:0, one launch (start us, length us, event | category | flops | bytes accessed | tf_op | source)
XLA Modules:
  0.0 105.7 jit_solution(8654785850193234521)
XLA Ops:
  0.0 5.1 %copy.12 = bf16[128,16,512]{0,1,2:T(8,128)(2,1)} copy(bf16[128,16,512]{2,1,0:T(8,128)(2,1)} %param.4) | data formatting | bytes 4194304 | tf_op args[0]
  5.1 0.0 copy-start.2
  5.1 0.0 copy-start.1
  5.1 7.4 %all-to-all-start = ((bf16[128,16,512]{0,1,2:T(8,128)(2,1)}), bf16[128,16,512]{0,1,2:T(8,128)(2,1)S(1)}, u32[]{:S(2)}, u32[]{:S(2)}) async-start(bf16[128,16,512]{0,1,2:T(8,128)(2,1)} %copy.12), calls=%async_computation | async-start | bytes 4194304 | tf_op jit(solution)/shard_map/all_to_all | solution.py:39
  12.5 0.0 copy-done.2
  12.5 0.0 copy-done.1
  12.5 0.2 cosine_convert_fusion
  12.7 48.0 %all-to-all-done = bf16[128,16,512]{0,1,2:T(8,128)(2,1)S(1)} async-done(((bf16[128,16,512]{0,1,2:T(8,128)(2,1)}), bf16[128,16,512]{0,1,2:T(8,128)(2,1)S(1)}, u32[]{:S(2)}, u32[]{:S(2)}) %all-to-all-start) | async-done | bytes 2097184 | tf_op jit(solution)/shard_map/all_to_all | solution.py:39
  60.7 2.7 %copy.14 = bf16[8,128,16,64]{1,0,3,2:T(8,128)(2,1)} copy(bf16[8,128,16,64]{1,2,3,0:T(8,128)(2,1)S(1)} %bitcast.39) | data formatting | bytes 4194304 | tf_op jit(solution)/shard_map/all_to_all | solution.py:39
  63.4 2.8 %all_to_all.16 = bf16[1024,16,64]{0,2,1:T(8,128)(2,1)S(1)} reshape(bf16[8,128,16,64]{1,0,3,2:T(8,128)(2,1)} %copy.14) | data formatting | bytes 4194304 | tf_op jit(solution)/shard_map/all_to_all | solution.py:39
  66.2 0.0 copy-start
  66.2 0.9 convolution_multiply_fusion
  67.2 1.9 %all_gather.3 = f32[2,2,32,64]{3,2,1,0:T(8,128)S(1)} all-gather(f32[2,2,16,64]{3,2,1,0:T(8,128)S(1)} %copy.15), channel_id=1, replica_groups=mesh['grp'=2,'wide'=8,'narrow'=2] {'narrow'}, dimensions={2}, use_global_device_ids=true | all-gather | bytes 49152 | tf_op jit(solution)/shard_map/all_gather | solution.py:48
  69.0 0.0 copy-done
  69.0 0.2 fusion.4
  69.2 35.2 %psum.7 = f32[2,2,16,32]{3,2,1,0:T(8,128)S(1)} all-reduce(f32[2,2,16,32]{3,2,1,0:T(8,128)S(1)} %fusion.4), channel_id=1, replica_groups=mesh['grp'=2,'wide'=8,'narrow'=2] {'wide'}, use_global_device_ids=true, to_apply=%region_0.1 | all-reduce | flops 2048 | bytes 16384 | tf_op jit(solution)/shard_map/psum | solution.py:47
  104.4 0.1 fusion.3
  104.6 0.2 fusion.2
  104.8 0.2 fusion
  104.9 0.2 fusion.1
  105.1 0.6 maximum_multiply_fusion
  (3 shorter events, 0.0 us)
Async XLA Ops:
  5.1 7.4 %copy-start.2 = (s32[16,1]{0,1:T(1,128)S(1)}, s32[16,1]{0,1:T(1,128)}, u32[]{:S(2)}) copy-start(s32[16,1]{0,1:T(1,128)} %param.5) | copy-start | bytes 196
  5.1 7.4 %copy-start.1 = (s32[2]{0:T(128)S(1)}, s32[2]{0:T(128)}, u32[]{:S(2)}) copy-start(s32[2]{0:T(128)} %param.7) | copy-start | bytes 28
  5.1 55.6 %all-to-all-start = ((bf16[128,16,512]{0,1,2:T(8,128)(2,1)}), bf16[128,16,512]{0,1,2:T(8,128)(2,1)S(1)}, u32[]{:S(2)}, u32[]{:S(2)}) async-start(bf16[128,16,512]{0,1,2:T(8,128)(2,1)} %copy.12), calls=%async_computation | async-start | bytes 4194304 | tf_op jit(solution)/shard_map/all_to_all | solution.py:39
  66.2 2.8 %copy-start = (s32[32]{0:T(128)S(1)}, s32[32]{0:T(128)}, u32[]{:S(2)}) copy-start(s32[32]{0:T(128)} %param.6) | copy-start | bytes 388
where the time goes:
time: 106 us
  waiting for transfers between devices  48 us (45%)
  blocking collectives  37.1 us (35%)
  local copies, waits for them, and re-layouts  10.6 us (10%)
  starting transfers between devices  7.38 us (7%)
  matrix products  1.75 us (2%)
    all_to_all x1, waiting for transfers between devices, shards(): lax.all_to_all(traces, 'wide', split_axis=2, concat_axis=0, tiled=True)  48 us
    psum x1, blocking collectives, shards(): coincident = lax.psum(local_part, 'wide')  35.2 us
    all_to_all x1, starting transfers between devices, shards(): lax.all_to_all(traces, 'wide', split_axis=2, concat_axis=0, tiled=True)  7.38 us
    all_to_all x2, local copies, waits for them, and re-layouts, shards(): lax.all_to_all(traces, 'wide', split_axis=2, concat_axis=0, tiled=True)  5.5 us
    unnamed x7, local copies, waits for them, and re-layouts  5.1 us
  transfers between devices with their start and end apart: 1, of which 1 were waited for; matrix products, arithmetic and copies ran while one was open for 0% of the time, Pallas kernels for 0%

commit v1 on v0

v1 whole, which is shorter than its diff:
```python
import functools
import math

import jax
import jax.numpy as jnp
from jax import lax
from jax.experimental import pallas as pl
from jax.experimental.pallas import tpu as pltpu
from jax.sharding import PartitionSpec as P

NT = 1024
RB = 512
LANES = 128
MESH = pl.DeviceIdType.MESH
F32 = jnp.float32
BF16 = jnp.bfloat16
SIN_TERMS = tuple((-1.0) ** i / math.factorial(2 * i + 1) for i in range(6))


def iota(shape, axis):
    return lax.broadcasted_iota(jnp.int32, shape, axis)


def each(count, body):
    if count <= 16:
        for i in range(count):
            body(i)
    else:
        lax.fori_loop(0, count, lambda i, c: (body(i), c)[1], 0)


def dft_block(freq_ref, first_time, shots, columns, first_column):
    shape = (8, columns)
    row = iota(shape, 0)
    lane = iota(shape, 1) + first_column
    freq = jnp.where(row % 2 == 0, freq_ref[0], freq_ref[1])
    m = freq * (first_time + lane // shots)
    m = (m + jnp.where(row >= 2, NT // 4, 0)) & (NT - 1)
    g = (m & (NT // 2 - 1)) - NT // 4
    x = g.astype(F32) * (2.0 * math.pi / NT)
    x2 = x * x
    acc = jnp.full(shape, SIN_TERMS[-1], F32)
    for term in SIN_TERMS[-2::-1]:
        acc = acc * x2 + term
    value = x * acc
    value = jnp.where(m >= NT // 2, value, -value)
    own = iota((shots, columns), 0) == iota((shots, columns), 1) % shots
    rows = [
        jnp.where(own, jnp.broadcast_to(value[j : j + 1], (shots, columns)), 0.0) for j in range(4)
    ]
    return jnp.concatenate(rows, axis=0).astype(BF16)


def kernel(
    n_wide, time_chunks,
    freq_ref, src_ref, aperture_ref, traces_ref, out_ref,
    x_ref, tx, rx, ctx, crx, stx, srx,
    load_sem, send_sem, recv_sem, csend_sem, crecv_sem, swap_sem,
):
    wide = lax.axis_index("wide")
    narrow = lax.axis_index("narrow")
    partner = 1 - narrow
    blocks, shots = aperture_ref.shape
    rows_total, receivers = traces_ref.shape
    rows = 4 * shots
    half = rows // 2
    recv_count = receivers // n_wide
    per_block = RB // recv_count
    sources = src_ref.shape[0]
    step = rows_total // time_chunks
    peers = n_wide - 1
    first = n_wide // 2

    def peer_of(i):
        return lax.rem(wide + 1 + lax.rem(first - 1 + i, peers), n_wide)

    def source_of(i):
        return lax.rem(wide + n_wide - 1 - lax.rem(first - 1 + i, peers), n_wide)

    barrier = pltpu.get_barrier_semaphore()
    each(peers, lambda i: pl.semaphore_signal(
        barrier, inc=1, device_id={"wide": peer_of(i)}, device_id_type=MESH))
    pl.semaphore_signal(barrier, inc=1, device_id={"narrow": partner}, device_id_type=MESH)

    loads = []
    for c in range(time_chunks):
        part = pl.ds(c * step, step)
        loads.append(pltpu.make_async_copy(traces_ref.at[part], x_ref.at[part], load_sem.at[c]))
        loads[-1].start()

    lane = iota((1, LANES), 1)
    lane_src = jnp.zeros((1, LANES), jnp.int32)
    for h in range(2):
        base = (narrow if h == 0 else partner) * shots
        for k in range(shots):
            at = (lane // rows == h) & (lane % shots == k)
            lane_src = jnp.where(at, src_ref[base + k], lane_src)
    first_time = wide * (rows_total // shots)
    tables = [dft_block(freq_ref, first_time, shots, step, c * step) for c in range(time_chunks)]

    low = iota((half, LANES), 1) < LANES // 2
    diagonal = iota((shots, shots), 0) == iota((shots, shots), 1)
    picked = None
    for b in range(blocks):
        raw = None
        for c in range(time_chunks):
            if b == 0:
                loads[c].wait()
            term = jnp.dot(
                tables[c],
                x_ref[c * step : (c + 1) * step, b * RB : (b + 1) * RB],
                preferred_element_type=F32,
            )
            raw = term if raw is None else raw + term
        flags = jnp.where(diagonal, aperture_ref[b : b + 1, :].astype(F32), 0.0)
        active = jnp.sum(flags, axis=1, keepdims=True) * NT ** (-0.5)
        spectra = raw * jnp.concatenate([active] * 4, axis=0)
        for p in range(per_block // 2):
            pair = spectra[:, p * LANES : (p + 1) * LANES]
            top, bottom = pair[:half], pair[half:]
            at = b * per_block + 2 * p
            tx[at] = jnp.where(low, top, pltpu.roll(bottom, LANES // 2, 1))
            tx[at + 1] = jnp.where(low, pltpu.roll(top, LANES // 2, 1), bottom)
        if b == blocks - 1:
            pl.semaphore_wait(barrier, peers + 1)

            def send(i):
                to = peer_of(i)
                pltpu.make_async_remote_copy(
                    src_ref=tx.at[to], dst_ref=rx.at[wide],
                    send_sem=send_sem.at[to], recv_sem=recv_sem.at[wide],
                    device_id={"wide": to}, device_id_type=MESH,
                ).start()

            each(peers, send)
        selector = (iota((RB, LANES), 0) + b * RB == lane_src).astype(F32).astype(BF16)
        hi = spectra.astype(BF16)
        rest = spectra - hi.astype(F32)
        mid = rest.astype(BF16)
        lo = (rest - mid.astype(F32)).astype(BF16)
        got = jnp.dot(jnp.concatenate([hi, mid, lo], axis=0), selector, preferred_element_type=F32)
        got = got[:rows] + got[rows : 2 * rows] + got[2 * rows :]
        picked = got if picked is None else picked + got

    kind = iota((shots, LANES), 1) // shots % 4
    packed = picked[:shots]
    for j in range(1, 4):
        packed = jnp.where(kind == j, picked[j * shots : (j + 1) * shots], packed)
    ctx[...] = packed

    def send_picked(i):
        to = peer_of(i)
        pltpu.make_async_remote_copy(
            src_ref=ctx, dst_ref=crx.at[wide],
            send_sem=csend_sem.at[to], recv_sem=crecv_sem.at[wide],
            device_id={"wide": to}, device_id_type=MESH,
        ).start()

    each(peers, send_picked)

    def copy_of(i):
        at = source_of(i)
        return pltpu.make_async_remote_copy(
            src_ref=tx.at[at], dst_ref=rx.at[at],
            send_sem=send_sem.at[at], recv_sem=recv_sem.at[at],
            device_id={"wide": at}, device_id_type=MESH,
        )

    def picked_copy_of(i):
        at = source_of(i)
        return pltpu.make_async_remote_copy(
            src_ref=ctx, dst_ref=crx.at[at],
            send_sem=csend_sem.at[at], recv_sem=crecv_sem.at[at],
            device_id={"wide": at}, device_id_type=MESH,
        )

    stx[...] = tx[wide]

    def add(i):
        copy_of(i).wait_recv()
        stx[...] += rx[source_of(i)]

    each(peers, add)
    swap = pltpu.make_async_remote_copy(
        src_ref=stx, dst_ref=srx, send_sem=swap_sem.at[0], recv_sem=swap_sem.at[1],
        device_id={"narrow": partner}, device_id_type=MESH,
    )
    swap.start()

    each(peers, lambda i: picked_copy_of(i).wait_recv())
    total = packed
    if peers <= 16:
        for i in range(peers):
            total = total + crx[source_of(i)]
    else:
        total = lax.fori_loop(0, peers, lambda i, c: c + crx[source_of(i)], total)
    total = total * sources ** (-0.5)
    quarter = LANES // 4
    part = iota((shots, LANES), 1) // quarter % 2
    swapped = jnp.where(
        part == 0, pltpu.roll(total, LANES - quarter, 1), pltpu.roll(total, quarter, 1)
    )
    signed = jnp.where(part == 0, total, -total)
    slice_of = iota((shots, LANES), 1) // shots % 2
    left = jnp.concatenate(
        [jnp.where(slice_of == q, v, 0.0) for v in (signed, swapped) for q in range(2)], axis=0
    )

    def spread(v):
        return jnp.concatenate([v[:, : LANES // 2], pltpu.roll(v, LANES // 2, 1)[:, : LANES // 2]], axis=0)

    result = jnp.dot(
        left[:, :rows], spread(stx[...]), preferred_element_type=F32, precision=lax.Precision.HIGHEST
    )
    swap.wait_recv()
    result = result + jnp.dot(
        left[:, rows:], spread(srx[...]), preferred_element_type=F32, precision=lax.Precision.HIGHEST
    )
    out_ref[...] = result.reshape(out_ref.shape)

    swap.wait_send()
    each(peers, lambda i: copy_of(i).wait_send())
    each(peers, lambda i: picked_copy_of(i).wait_send())


def solution(mesh):
    n_wide = mesh.shape["wide"]

    def shards(traces, aperture, source_points, freq_idx):
        times, shots, receivers = traces.shape
        recv_count = receivers // n_wide
        assert 2 * recv_count == LANES and 8 * shots == LANES
        assert mesh.shape["narrow"] == 2 and source_points.shape[0] == 2 * shots
        time_chunks = 4 if times % 32 == 0 else 1
        return pl.pallas_call(
            functools.partial(kernel, n_wide, time_chunks),
            out_shape=jax.ShapeDtypeStruct((2, 2, shots, recv_count), F32),
            in_specs=[
                pl.BlockSpec(memory_space=pltpu.SMEM),
                pl.BlockSpec(memory_space=pltpu.SMEM),
                pl.BlockSpec(memory_space=pltpu.VMEM),
                pl.BlockSpec(memory_space=pl.ANY),
            ],
            out_specs=pl.BlockSpec(memory_space=pltpu.VMEM),
            scratch_shapes=[
                pltpu.VMEM((times * shots, receivers), BF16),
                pltpu.VMEM((n_wide, 2 * shots, LANES), F32),
                pltpu.VMEM((n_wide, 2 * shots, LANES), F32),
                pltpu.VMEM((shots, LANES), F32),
                pltpu.VMEM((n_wide, shots, LANES), F32),
                pltpu.VMEM((2 * shots, LANES), F32),
                pltpu.VMEM((2 * shots, LANES), F32),
                pltpu.SemaphoreType.DMA((time_chunks,)),
                pltpu.SemaphoreType.DMA((n_wide,)),
                pltpu.SemaphoreType.DMA((n_wide,)),
                pltpu.SemaphoreType.DMA((n_wide,)),
                pltpu.SemaphoreType.DMA((n_wide,)),
                pltpu.SemaphoreType.DMA((2,)),
            ],
            compiler_params=pltpu.CompilerParams(
                collective_id=0, has_side_effects=True, vmem_limit_bytes=60 * 2**20
            ),
        )(freq_idx, source_points, aperture.T, traces.reshape(times * shots, receivers))

    placed = (P("wide", ("grp", "narrow"), None), P(("grp", "narrow"), None), P("grp"), P())
    return jax.shard_map(
        shards,
        mesh=mesh,
        in_specs=placed,
        out_specs=P(None, None, ("grp", "narrow"), "wide"),
        check_vma=False,
    )
```

time: 106 us -> 15.4 us (0.15)
  waiting for transfers between devices: 48 us -> 0 us
  blocking collectives: 37.1 us -> 0 us
  Pallas kernels: 0 us -> 13.8 us
  local copies, waits for them, and re-layouts: 10.6 us -> 1.38 us
  starting transfers between devices: 7.38 us -> 0 us
  matrix products: 1.75 us -> 0 us
    all_to_all x1 -> x0, waiting for transfers between devices: 48 us -> none  [shards(): lax.all_to_all(traces, 'wide', split_axis=2, concat_axis=0, tiled=True)]
    psum x1 -> x0, blocking collectives: 35.2 us -> none  [shards(): coincident = lax.psum(local_part, 'wide')]
    pallas_call x0 -> x1, Pallas kernels: none -> 13.8 us  [shards(): pl.pallas_call(functools.partial(kernel, n_wide, time_chunks), out_shape=...]
    all_to_all x1 -> x0, starting transfers between devices: 7.38 us -> none  [shards(): lax.all_to_all(traces, 'wide', split_axis=2, concat_axis=0, tiled=True)]
    all_to_all x2 -> x0, local copies, waits for them, and re-layouts: 5.5 us -> none  [shards(): lax.all_to_all(traces, 'wide', split_axis=2, concat_axis=0, tiled=True)]
    unnamed x7 -> x1, local copies, waits for them, and re-layouts: 5.1 us -> 1.38 us
    all_gather x1 -> x0, blocking collectives: 1.86 us -> none  [shards(): all_shot_records = lax.all_gather(spectra, 'narrow', axis=2, tiled=True)]
    dot_general x6 -> x0, matrix products: 1.75 us -> none  [the longest x1 0.91 us: apply_table(): jnp.einsum('ua,aid->uid', fourier_table, column_entries, preferred_elemen...]
  transfers between devices with their start and end apart: 1 -> 0, of which waited for: 1 -> 0; matrix products, arithmetic and copies ran while one was open for 0% -> 0% of each run, Pallas kernels for 0% -> 0%
where the time goes in v1:
time: 15.4 us; the launch traced here: 15.2 us
  Pallas kernels  13.8 us (90%)
  local copies, waits for them, and re-layouts  1.38 us (9%)
    pallas_call x1, Pallas kernels, shards(): pl.pallas_call(functools.partial(kernel, n_wide, time_chunks), out_shape=...  13.8 us
    unnamed x1, local copies, waits for them, and re-layouts  1.38 us

profile of v1, /device:TPU:0, one launch (start us, length us, event | category | flops | bytes accessed | tf_op | source)
XLA Modules:
  0.0 15.2 jit_solution(6136073664363031878)
XLA Ops:
  0.0 13.8 %shard_map.46 = f32[2,2,16,64]{3,2,1,0:T(8,128)} custom-call(s32[2]{0:T(128)} %freq_ref.1, s32[32]{0:T(128)} %src_ref.1, s32[1,16]{1,0:T(1,128)} %bitcast.3, bf16[2048,512]{1,0:T(8,128)(2,1)} %bitcast.2), custom_call_target="tpu_custom_call" | custom-call | tf_op jit(solution)/shard_map/pallas_call | solution.py:235
  13.8 1.4 %copy.6 = f32[2,2,16,64]{3,2,1,0:T(8,128)} copy(f32[2,2,16,64]{3,2,1,0:T(8,128)} %shard_map.46) | data formatting | bytes 32768

commit v2 on v1

--- a/solution.py
+++ b/solution.py
@@ -52,10 +52,10 @@
 
 
 def kernel(
-    n_wide, time_chunks,
-    freq_ref, src_ref, aperture_ref, traces_ref, out_ref,
-    x_ref, tx, rx, ctx, crx, stx, srx,
-    load_sem, send_sem, recv_sem, csend_sem, crecv_sem, swap_sem,
+    n_wide, width,
+    freq_hbm, src_hbm, aperture_hbm, traces_ref, out_ref,
+    freq_ref, src_ref, aperture_ref, x_ref, tx, rx, ctx, crx, stx, srx,
+    small_sem, load_sem, send_sem, recv_sem, csend_sem, crecv_sem, swap_sem,
 ):
     wide = lax.axis_index("wide")
     narrow = lax.axis_index("narrow")
@@ -65,28 +65,35 @@
     rows = 4 * shots
     half = rows // 2
     recv_count = receivers // n_wide
-    per_block = RB // recv_count
-    sources = src_ref.shape[0]
-    step = rows_total // time_chunks
+    pieces = receivers // width
     peers = n_wide - 1
-    first = n_wide // 2
 
     def peer_of(i):
-        return lax.rem(wide + 1 + lax.rem(first - 1 + i, peers), n_wide)
-
-    def source_of(i):
-        return lax.rem(wide + n_wide - 1 - lax.rem(first - 1 + i, peers), n_wide)
+        return i + jnp.where(wide <= i, 1, 0)
 
     barrier = pltpu.get_barrier_semaphore()
     each(peers, lambda i: pl.semaphore_signal(
         barrier, inc=1, device_id={"wide": peer_of(i)}, device_id_type=MESH))
     pl.semaphore_signal(barrier, inc=1, device_id={"narrow": partner}, device_id_type=MESH)
 
-    loads = []
-    for c in range(time_chunks):
-        part = pl.ds(c * step, step)
-        loads.append(pltpu.make_async_copy(traces_ref.at[part], x_ref.at[part], load_sem.at[c]))
-        loads[-1].start()
+    smalls = [
+        pltpu.make_async_copy(here, there, small_sem.at[i])
+        for i, (here, there) in enumerate(
+            ((freq_hbm, freq_ref), (src_hbm, src_ref), (aperture_hbm, aperture_ref))
+        )
+    ]
+    for copy in smalls:
+        copy.start()
+    loads = [
+        pltpu.make_async_copy(
+            traces_ref.at[:, pl.ds(c * width, width)], x_ref.at[c], load_sem.at[c]
+        )
+        for c in range(pieces)
+    ]
+    for copy in loads:
+        copy.start()
+    for copy in smalls:
+        copy.wait()
 
     lane = iota((1, LANES), 1)
     lane_src = jnp.zeros((1, LANES), jnp.int32)
@@ -96,44 +103,41 @@
             at = (lane // rows == h) & (lane % shots == k)
             lane_src = jnp.where(at, src_ref[base + k], lane_src)
     first_time = wide * (rows_total // shots)
-    tables = [dft_block(freq_ref, first_time, shots, step, c * step) for c in range(time_chunks)]
+    table = dft_block(freq_ref, first_time, shots, rows_total, 0)
 
     low = iota((half, LANES), 1) < LANES // 2
     diagonal = iota((shots, shots), 0) == iota((shots, shots), 1)
     picked = None
-    for b in range(blocks):
-        raw = None
-        for c in range(time_chunks):
-            if b == 0:
-                loads[c].wait()
-            term = jnp.dot(
-                tables[c],
-                x_ref[c * step : (c + 1) * step, b * RB : (b + 1) * RB],
-                preferred_element_type=F32,
-            )
-            raw = term if raw is None else raw + term
+    def send(to):
+        @pl.when(to != wide)
+        def _():
+            pltpu.make_async_remote_copy(
+                src_ref=tx.at[to], dst_ref=rx.at[wide],
+                send_sem=send_sem.at[to], recv_sem=recv_sem.at[wide],
+                device_id={"wide": to}, device_id_type=MESH,
+            ).start()
+
+    def active_of(b):
         flags = jnp.where(diagonal, aperture_ref[b : b + 1, :].astype(F32), 0.0)
         active = jnp.sum(flags, axis=1, keepdims=True) * NT ** (-0.5)
-        spectra = raw * jnp.concatenate([active] * 4, axis=0)
-        for p in range(per_block // 2):
+        return jnp.concatenate([active] * 4, axis=0)
+
+    actives = [active_of(b) for b in range(blocks)]
+    for c in range(pieces):
+        loads[c].wait()
+        raw = jnp.dot(table, x_ref[c], preferred_element_type=F32)
+        spectra = raw * actives[c * width // RB]
+        per_piece = width // recv_count
+        for p in range(per_piece // 2):
             pair = spectra[:, p * LANES : (p + 1) * LANES]
             top, bottom = pair[:half], pair[half:]
-            at = b * per_block + 2 * p
+            at = c * per_piece + 2 * p
             tx[at] = jnp.where(low, top, pltpu.roll(bottom, LANES // 2, 1))
             tx[at + 1] = jnp.where(low, pltpu.roll(top, LANES // 2, 1), bottom)
-        if b == blocks - 1:
+        if c == 0:
             pl.semaphore_wait(barrier, peers + 1)
-
-            def send(i):
-                to = peer_of(i)
-                pltpu.make_async_remote_copy(
-                    src_ref=tx.at[to], dst_ref=rx.at[wide],
-                    send_sem=send_sem.at[to], recv_sem=recv_sem.at[wide],
-                    device_id={"wide": to}, device_id_type=MESH,
-                ).start()
-
-            each(peers, send)
-        selector = (iota((RB, LANES), 0) + b * RB == lane_src).astype(F32).astype(BF16)
+        each(per_piece, lambda i: send(c * per_piece + i))
+        selector = (iota((width, LANES), 0) + c * width == lane_src).astype(F32).astype(BF16)
         hi = spectra.astype(BF16)
         rest = spectra - hi.astype(F32)
         mid = rest.astype(BF16)
@@ -159,7 +163,7 @@
     each(peers, send_picked)
 
     def copy_of(i):
-        at = source_of(i)
+        at = peer_of(i)
         return pltpu.make_async_remote_copy(
             src_ref=tx.at[at], dst_ref=rx.at[at],
             send_sem=send_sem.at[at], recv_sem=recv_sem.at[at],
@@ -167,7 +171,7 @@
         )
 
     def picked_copy_of(i):
-        at = source_of(i)
+        at = peer_of(i)
         return pltpu.make_async_remote_copy(
             src_ref=ctx, dst_ref=crx.at[at],
             send_sem=csend_sem.at[at], recv_sem=crecv_sem.at[at],
@@ -178,7 +182,7 @@
 
     def add(i):
         copy_of(i).wait_recv()
-        stx[...] += rx[source_of(i)]
+        stx[...] += rx[peer_of(i)]
 
     each(peers, add)
     swap = pltpu.make_async_remote_copy(
@@ -191,10 +195,9 @@
     total = packed
     if peers <= 16:
         for i in range(peers):
-            total = total + crx[source_of(i)]
+            total = total + crx[peer_of(i)]
     else:
-        total = lax.fori_loop(0, peers, lambda i, c: c + crx[source_of(i)], total)
-    total = total * sources ** (-0.5)
+        total = lax.fori_loop(0, peers, lambda i, c: c + crx[peer_of(i)], total)
     quarter = LANES // 4
     part = iota((shots, LANES), 1) // quarter % 2
     swapped = jnp.where(
@@ -231,26 +234,26 @@
         recv_count = receivers // n_wide
         assert 2 * recv_count == LANES and 8 * shots == LANES
         assert mesh.shape["narrow"] == 2 and source_points.shape[0] == 2 * shots
-        time_chunks = 4 if times % 32 == 0 else 1
-        return pl.pallas_call(
-            functools.partial(kernel, n_wide, time_chunks),
-            out_shape=jax.ShapeDtypeStruct((2, 2, shots, recv_count), F32),
-            in_specs=[
-                pl.BlockSpec(memory_space=pltpu.SMEM),
-                pl.BlockSpec(memory_space=pltpu.SMEM),
-                pl.BlockSpec(memory_space=pltpu.VMEM),
-                pl.BlockSpec(memory_space=pl.ANY),
-            ],
+        width = LANES if n_wide <= 16 else RB
+        pieces = receivers // width
+        products = pl.pallas_call(
+            functools.partial(kernel, n_wide, width),
+            out_shape=pltpu.VMEM((2, 2, shots, recv_count), F32),
+            in_specs=[pl.BlockSpec(memory_space=pltpu.HBM)] * 4,
             out_specs=pl.BlockSpec(memory_space=pltpu.VMEM),
             scratch_shapes=[
-                pltpu.VMEM((times * shots, receivers), BF16),
+                pltpu.SMEM(freq_idx.shape, jnp.int32),
+                pltpu.SMEM(source_points.shape, jnp.int32),
+                pltpu.VMEM(aperture.shape[::-1], jnp.int32),
+                pltpu.VMEM((pieces, times * shots, width), BF16),
                 pltpu.VMEM((n_wide, 2 * shots, LANES), F32),
                 pltpu.VMEM((n_wide, 2 * shots, LANES), F32),
                 pltpu.VMEM((shots, LANES), F32),
                 pltpu.VMEM((n_wide, shots, LANES), F32),
                 pltpu.VMEM((2 * shots, LANES), F32),
                 pltpu.VMEM((2 * shots, LANES), F32),
-                pltpu.SemaphoreType.DMA((time_chunks,)),
+                pltpu.SemaphoreType.DMA((3,)),
+                pltpu.SemaphoreType.DMA((pieces,)),
                 pltpu.SemaphoreType.DMA((n_wide,)),
                 pltpu.SemaphoreType.DMA((n_wide,)),
                 pltpu.SemaphoreType.DMA((n_wide,)),
@@ -261,6 +264,7 @@
                 collective_id=0, has_side_effects=True, vmem_limit_bytes=60 * 2**20
             ),
         )(freq_idx, source_points, aperture.T, traces.reshape(times * shots, receivers))
+        return products * source_points.shape[0] ** (-0.5)
 
     placed = (P("wide", ("grp", "narrow"), None), P(("grp", "narrow"), None), P("grp"), P())
     return jax.shard_map(

time: 15.4 us -> 12.9 us (0.84)
  Pallas kernels: 13.8 us -> 12.1 us
  local copies, waits for them, and re-layouts: 1.38 us -> 0 us
  other arithmetic: 0 us -> 0.62 us
    pallas_call x1, Pallas kernels: 13.8 us -> 12.1 us  [shards(): pl.pallas_call(functools.partial(kernel, n_wide, width), out_shape=pltpu....]
    unnamed x1 -> x0, local copies, waits for them, and re-layouts: 1.38 us -> none
    mul x0 -> x1, other arithmetic: none -> 0.62 us  [shards(): return products * source_points.shape[0] ** (-0.5)]
where the time goes in v2:
time: 12.9 us; the launch traced here: 12.7 us
  Pallas kernels  12.1 us (94%)
  other arithmetic  0.62 us (5%)
    pallas_call x1, Pallas kernels, shards(): pl.pallas_call(functools.partial(kernel, n_wide, width), out_shape=pltpu....  12.1 us
    mul x1, other arithmetic, shards(): return products * source_points.shape[0] ** (-0.5)  0.62 us

profile of v2, /device:TPU:0, one launch (start us, length us, event | category | flops | bytes accessed | tf_op | source)
XLA Modules:
  0.0 12.7 jit_solution(6067941688058294766)
XLA Ops:
  0.0 12.1 %shard_map.46 = f32[2,2,16,64]{3,2,1,0:T(8,128)S(1)} custom-call(s32[2]{0:T(128)} %freq_hbm.1, s32[32]{0:T(128)} %src_hbm.1, s32[1,16]{1,0:T(1,128)} %bitcast.3, bf16[2048,512]{1,0:T(8,128)(2,1)} %bitcast.2), custom_call_target="tpu_custom_call" | custom-call | tf_op jit(solution)/shard_map/pallas_call | solution.py:239
  12.1 0.6 %broadcast_multiply_fusion = f32[2,2,16,64]{3,2,1,0:T(8,128)} fusion(f32[2,2,16,64]{3,2,1,0:T(8,128)S(1)} %shard_map.46), kind=kLoop, calls=%fused_computation | loop fusion | flops 4096 | bytes 32768 | tf_op jit(solution)/shard_map/mul | solution.py:267

commit v3 on v2

--- a/solution.py
+++ b/solution.py
@@ -55,7 +55,7 @@
     n_wide, width,
     freq_hbm, src_hbm, aperture_hbm, traces_ref, out_ref,
     freq_ref, src_ref, aperture_ref, x_ref, tx, rx, ctx, crx, stx, srx,
-    small_sem, load_sem, send_sem, recv_sem, csend_sem, crecv_sem, swap_sem,
+    small_sem, load_sem, send_sem, recv_sem, csend_sem, crecv_sem, swap_sem, ready_sem,
 ):
     wide = lax.axis_index("wide")
     narrow = lax.axis_index("narrow")
@@ -72,8 +72,20 @@
         return i + jnp.where(wide <= i, 1, 0)
 
     barrier = pltpu.get_barrier_semaphore()
-    each(peers, lambda i: pl.semaphore_signal(
-        barrier, inc=1, device_id={"wide": peer_of(i)}, device_id_type=MESH))
+
+    def announce(to):
+        @pl.when(to > wide)
+        def _():
+            pl.semaphore_signal(barrier, inc=1, device_id={"wide": to}, device_id_type=MESH)
+
+    def answer(to):
+        @pl.when(to < wide)
+        def _():
+            pl.semaphore_signal(
+                ready_sem.at[wide], inc=1, device_id={"wide": to}, device_id_type=MESH
+            )
+
+    each(n_wide, announce)
     pl.semaphore_signal(barrier, inc=1, device_id={"narrow": partner}, device_id_type=MESH)
 
     smalls = [
@@ -92,6 +104,8 @@
     ]
     for copy in loads:
         copy.start()
+    pl.semaphore_wait(barrier, wide + 1)
+    each(n_wide, answer)
     for copy in smalls:
         copy.wait()
 
@@ -108,14 +122,17 @@
     low = iota((half, LANES), 1) < LANES // 2
     diagonal = iota((shots, shots), 0) == iota((shots, shots), 1)
     picked = None
-    def send(to):
-        @pl.when(to != wide)
-        def _():
-            pltpu.make_async_remote_copy(
-                src_ref=tx.at[to], dst_ref=rx.at[wide],
-                send_sem=send_sem.at[to], recv_sem=recv_sem.at[wide],
-                device_id={"wide": to}, device_id_type=MESH,
-            ).start()
+    def spectra_to(to):
+        return pltpu.make_async_remote_copy(
+            src_ref=tx.at[to], dst_ref=rx.at[wide],
+            send_sem=send_sem.at[to], recv_sem=recv_sem.at[wide],
+            device_id={"wide": to}, device_id_type=MESH,
+        )
+
+    def send_below(to):
+        @pl.when(to < wide)
+        def _():
+            spectra_to(to).start()
 
     def active_of(b):
         flags = jnp.where(diagonal, aperture_ref[b : b + 1, :].astype(F32), 0.0)
@@ -135,8 +152,7 @@
             tx[at] = jnp.where(low, top, pltpu.roll(bottom, LANES // 2, 1))
             tx[at + 1] = jnp.where(low, pltpu.roll(top, LANES // 2, 1), bottom)
         if c == 0:
-            pl.semaphore_wait(barrier, peers + 1)
-        each(per_piece, lambda i: send(c * per_piece + i))
+            each(per_piece, send_below)
         selector = (iota((width, LANES), 0) + c * width == lane_src).astype(F32).astype(BF16)
         hi = spectra.astype(BF16)
         rest = spectra - hi.astype(F32)
@@ -152,15 +168,24 @@
         packed = jnp.where(kind == j, picked[j * shots : (j + 1) * shots], packed)
     ctx[...] = packed
 
-    def send_picked(i):
+    def send_rest(i):
         to = peer_of(i)
+
+        @pl.when(to > wide)
+        def _():
+            pl.semaphore_wait(ready_sem.at[to], 1)
+
+        @pl.when((to > wide) | (to >= width // recv_count))
+        def _():
+            spectra_to(to).start()
+
         pltpu.make_async_remote_copy(
             src_ref=ctx, dst_ref=crx.at[wide],
             send_sem=csend_sem.at[to], recv_sem=crecv_sem.at[wide],
             device_id={"wide": to}, device_id_type=MESH,
         ).start()
 
-    each(peers, send_picked)
+    each(peers, send_rest)
 
     def copy_of(i):
         at = peer_of(i)
@@ -259,6 +284,7 @@
                 pltpu.SemaphoreType.DMA((n_wide,)),
                 pltpu.SemaphoreType.DMA((n_wide,)),
                 pltpu.SemaphoreType.DMA((2,)),
+                pltpu.SemaphoreType.REGULAR((n_wide,)),
             ],
             compiler_params=pltpu.CompilerParams(
                 collective_id=0, has_side_effects=True, vmem_limit_bytes=60 * 2**20

time: 12.9 us -> 12.1 us (0.938)
  Pallas kernels: 12.1 us -> 11.4 us
    pallas_call x1, Pallas kernels: 12.1 us -> 11.4 us  [shards(): pl.pallas_call(functools.partial(kernel, n_wide, width), out_shape=pltpu....]
where the time goes in v3:
time: 12.1 us; the launch traced here: 12 us
  Pallas kernels  11.4 us (94%)
  other arithmetic  0.62 us (5%)
    pallas_call x1, Pallas kernels, shards(): pl.pallas_call(functools.partial(kernel, n_wide, width), out_shape=pltpu....  11.4 us
    mul x1, other arithmetic, shards(): return products * source_points.shape[0] ** (-0.5)  0.62 us

profile of v3, /device:TPU:0, one launch (start us, length us, event | category | flops | bytes accessed | tf_op | source)
XLA Modules:
  0.0 12.0 jit_solution(9949514492311720939)
XLA Ops:
  0.0 11.4 %shard_map.46 = f32[2,2,16,64]{3,2,1,0:T(8,128)S(1)} custom-call(s32[2]{0:T(128)} %freq_hbm.1, s32[32]{0:T(128)} %src_hbm.1, s32[1,16]{1,0:T(1,128)} %bitcast.3, bf16[2048,512]{1,0:T(8,128)(2,1)} %bitcast.2), custom_call_target="tpu_custom_call" | custom-call | tf_op jit(solution)/shard_map/pallas_call | solution.py:264
  11.4 0.6 %broadcast_multiply_fusion = f32[2,2,16,64]{3,2,1,0:T(8,128)} fusion(f32[2,2,16,64]{3,2,1,0:T(8,128)S(1)} %shard_map.46), kind=kLoop, calls=%fused_computation | loop fusion | flops 4096 | bytes 32768 | tf_op jit(solution)/shard_map/mul | solution.py:293

commit v4 on v3

--- a/solution.py
+++ b/solution.py
@@ -96,11 +96,15 @@
     ]
     for copy in smalls:
         copy.start()
+    deep = rows_total // 2
     loads = [
         pltpu.make_async_copy(
-            traces_ref.at[:, pl.ds(c * width, width)], x_ref.at[c], load_sem.at[c]
+            traces_ref.at[pl.ds(r * deep, deep), pl.ds(c * width, width)],
+            x_ref.at[c, pl.ds(r * deep, deep)],
+            load_sem.at[2 * c + r],
         )
         for c in range(pieces)
+        for r in range(2)
     ]
     for copy in loads:
         copy.start()
@@ -141,7 +145,8 @@
 
     actives = [active_of(b) for b in range(blocks)]
     for c in range(pieces):
-        loads[c].wait()
+        loads[2 * c].wait()
+        loads[2 * c + 1].wait()
         raw = jnp.dot(table, x_ref[c], preferred_element_type=F32)
         spectra = raw * actives[c * width // RB]
         per_piece = width // recv_count
@@ -278,7 +283,7 @@
                 pltpu.VMEM((2 * shots, LANES), F32),
                 pltpu.VMEM((2 * shots, LANES), F32),
                 pltpu.SemaphoreType.DMA((3,)),
-                pltpu.SemaphoreType.DMA((pieces,)),
+                pltpu.SemaphoreType.DMA((2 * pieces,)),
                 pltpu.SemaphoreType.DMA((n_wide,)),
                 pltpu.SemaphoreType.DMA((n_wide,)),
                 pltpu.SemaphoreType.DMA((n_wide,)),

time: 12.1 us -> 12.3 us (1.017)
  no operation moved by 1% of the time
where the time goes in v4:
time: 12.3 us; the launch traced here: 12.1 us
  Pallas kernels  11.5 us (93%)
  other arithmetic  0.62 us (5%)
    pallas_call x1, Pallas kernels, shards(): pl.pallas_call(functools.partial(kernel, n_wide, width), out_shape=pltpu....  11.5 us
    mul x1, other arithmetic, shards(): return products * source_points.shape[0] ** (-0.5)  0.62 us

profile of v4, /device:TPU:0, one launch (start us, length us, event | category | flops | bytes accessed | tf_op | source)
XLA Modules:
  0.0 12.1 jit_solution(12101547500465113581)
XLA Ops:
  0.0 11.5 %shard_map.46 = f32[2,2,16,64]{3,2,1,0:T(8,128)S(1)} custom-call(s32[2]{0:T(128)} %freq_hbm.1, s32[32]{0:T(128)} %src_hbm.1, s32[1,16]{1,0:T(1,128)} %bitcast.3, bf16[2048,512]{1,0:T(8,128)(2,1)} %bitcast.2), custom_call_target="tpu_custom_call" | custom-call | tf_op jit(solution)/shard_map/pallas_call | solution.py:269
  11.5 0.6 %broadcast_multiply_fusion = f32[2,2,16,64]{3,2,1,0:T(8,128)} fusion(f32[2,2,16,64]{3,2,1,0:T(8,128)S(1)} %shard_map.46), kind=kLoop, calls=%fused_computation | loop fusion | flops 4096 | bytes 32768 | tf_op jit(solution)/shard_map/mul | solution.py:298
